TPU v7x, 32 devices: a whole 2x2x4 slice. The times are simulated.
32 devices in a mesh: gx: 4 (over z), gy: 2 (over y), gz: 4 (over x, core).
Axes of the slice: x: 2, y: 2, z: 4, core: 2. Of those that a mesh axis runs over, the one named last changes fastest.
Arguments:
- e_field: float32 [3, 32, 128, 256], P(None, 'gx', 'gz', 'gy'), may hold values from -6 to 6
- h_field: float32 [3, 32, 128, 256], P(None, 'gx', 'gz', 'gy'), may hold values from -6 to 6
- e_forward: float32 [3, 32, 128, 256], P(None, 'gx', 'gz', 'gy'), may hold values from -6 to 6
- e_coeff: float32 [32, 128, 256], P('gx', 'gz', 'gy'), may hold values from 0.1 to 0.5
- h_coeff: float32 [32, 128, 256], P('gx', 'gz', 'gy'), may hold values from 0.1 to 0.5
- dft_acc: float32 [16, 32, 128, 256], P(None, 'gx', 'gz', 'gy'), may hold values from -6 to 6
- design_mask: int32 [4, 4, 32], P('gx', 'gz', 'gy'), may hold values 0 or 1
- omega_t: float32 [8], replicated, may hold values from -3.140625 to 3.140625
- port_index: int32 [4], replicated, may hold values from 0 to 31
- port_owner: int32 [4], replicated, may hold values from 0 to 31
- port_modes: float32 [4, 2, 128, 256], P(None, None, 'gz', 'gy'), may hold values from -0.0234375 to 0.0234375
- monitor_acc: float32 [32, 16], P(('gx', 'gy', 'gz')), may hold values from -6 to 6
Outputs:
- e_next: float32 [3, 32, 128, 256], P(None, 'gx', 'gz', 'gy')
- h_next: float32 [3, 32, 128, 256], P(None, 'gx', 'gz', 'gy')
- dft_next: float32 [16, 32, 128, 256], P(None, 'gx', 'gz', 'gy')
- monitor_next: float32 [32, 16], P(('gx', 'gy', 'gz'))
All inputs are finite; a program needn't handle non-finite values. No bound on the sum of `design_mask` on one device may be relied on, other than what follows from the above.
Results may differ from a plain program's by a relative error of at most 0.00011.
Values sent between devices are 32-bit elements; how exact they have to be, the bound alone decides.
A program may use at most 64 MiB of HBM per device.

v0:
```python
import jax
import jax.numpy as jnp
from jax import lax
from jax.sharding import PartitionSpec as P

BX = 8
BY = 8
BZ = 32


def from_behind(x, axis, by):
    length = lax.axis_size(axis)
    pairs = [(i, i + by) for i in range(length) if 0 <= i + by < length]
    return lax.ppermute(x, axis, pairs)


def lower_diff(field, below, along):
    size = field.shape[along]
    before = jnp.concatenate([below, lax.slice_in_dim(field, 0, size - 1, axis=along)], along)
    return field - before


def upper_diff(field, above, along):
    size = field.shape[along]
    after = jnp.concatenate([lax.slice_in_dim(field, 1, size, axis=along), above], along)
    return after - field


def face_gx(planes, offset):
    return from_behind(planes, "gx", offset)


def face_gy(planes, offset):
    return from_behind(planes, "gy", offset)


def face_gz(planes, offset):
    return from_behind(planes, "gz", offset)


def body(
    e_field,
    h_field,
    e_forward,
    e_coeff,
    h_coeff,
    dft_acc,
    design_mask,
    omega_t,
    port_index,
    port_owner,
    port_modes,
    monitor_acc,
):
    below_x = face_gx(h_field[1:3, -1:], 1)
    below_y = face_gy(jnp.stack([h_field[0, :, :, -1:], h_field[2, :, :, -1:]]), 1)
    below_z = face_gz(h_field[0:2, :, -1:], 1)
    curl_h = jnp.stack(
        [
            lower_diff(h_field[2], below_y[1], 2) - lower_diff(h_field[1], below_z[1], 1),
            lower_diff(h_field[0], below_z[0], 1) - lower_diff(h_field[2], below_x[1], 0),
            lower_diff(h_field[1], below_x[0], 0) - lower_diff(h_field[0], below_y[0], 2),
        ]
    )
    e_next = e_field - e_coeff[None] * curl_h
    above_x = face_gx(e_next[1:3, :1], -1)
    above_y = face_gy(jnp.stack([e_next[0, :, :, :1], e_next[2, :, :, :1]]), -1)
    above_z = face_gz(e_next[0:2, :, :1], -1)
    curl_e = jnp.stack(
        [
            upper_diff(e_next[2], above_y[1], 2) - upper_diff(e_next[1], above_z[1], 1),
            upper_diff(e_next[0], above_z[0], 1) - upper_diff(e_next[2], above_x[1], 0),
            upper_diff(e_next[1], above_x[0], 0) - upper_diff(e_next[0], above_y[0], 2),
        ]
    )
    h_next = h_field + h_coeff[None] * curl_e
    cells_x, cells_z, cells_y = e_coeff.shape
    bricks_x, bricks_z, bricks_y = design_mask.shape
    cosines = jnp.cos(omega_t)
    sines = jnp.sin(omega_t)
    phase = jnp.concatenate([cosines, -sines])
    brick_weight = design_mask.astype(jnp.float32)[:, None, :, None, :, None]
    dotted = jnp.sum(e_forward * e_next, axis=0).reshape(bricks_x, BX, bricks_z, BZ, bricks_y, BY)
    product = (brick_weight * dotted).reshape(cells_x, cells_z, cells_y)
    dft_next = dft_acc + phase[:, None, None, None] * product[None]
    first_x = lax.axis_index("gx") * cells_x
    selector = (
        port_index[:, None] == first_x + jnp.arange(cells_x, dtype=jnp.int32)[None, :]
    ).astype(jnp.float32)
    planes_y = jnp.einsum("px,xzy->pzy", selector, e_next[1], precision=lax.Precision.HIGHEST)
    planes_z = jnp.einsum("px,xzy->pzy", selector, e_next[2], precision=lax.Precision.HIGHEST)
    partial_intersection = jnp.sum(
        port_modes[:, 0] * planes_y + port_modes[:, 1] * planes_z, axis=(1, 2)
    )
    devices = lax.axis_size(("gx", "gy", "gz"))
    owned = (port_owner[None, :] == jnp.arange(devices, dtype=jnp.int32)[:, None]).astype(
        jnp.float32
    )
    terms = jnp.dot(
        owned, partial_intersection[:, None] * phase[None, :], precision=lax.Precision.HIGHEST
    )
    monitor_next = monitor_acc + lax.psum_scatter(
        terms, ("gx", "gy", "gz"), scatter_dimension=0, tiled=True
    )
    return (e_next, h_next, dft_next, monitor_next)


def solution(mesh):
    in_specs = (
        P(None, "gx", "gz", "gy"),
        P(None, "gx", "gz", "gy"),
        P(None, "gx", "gz", "gy"),
        P("gx", "gz", "gy"),
        P("gx", "gz", "gy"),
        P(None, "gx", "gz", "gy"),
        P("gx", "gz", "gy"),
        P(),
        P(),
        P(),
        P(None, None, "gz", "gy"),
        P(("gx", "gy", "gz"), None),
    )
    out_specs = (
        P(None, "gx", "gz", "gy"),
        P(None, "gx", "gz", "gy"),
        P(None, "gx", "gz", "gy"),
        P(("gx", "gy", "gz"), None),
    )
    return jax.shard_map(body, mesh=mesh, in_specs=in_specs, out_specs=out_specs, check_vma=False)
```

profile of v0, /device:TPU:0, one launch (start us, length us, event | category | flops | bytes accessed | tf_op | source)
XLA Modules:
  0.0 77.0 jit_solution(18215437652994910328)
XLA Ops:
  0.6 0.0 copy-start.13
  0.6 0.0 copy-start.14
  0.7 0.0 copy-start.7
  0.7 0.8 %slice.148 = f32[2,1,32,128]{3,2,1,0:T(8,128)S(1)} slice(f32[3,8,32,128]{3,2,1,0:T(8,128)} %param.13), slice={[1:3], [7:8], [0:32], [0:128]} | slice | bytes 65536 | tf_op jit(solution)/shard_map/slice | solution.py:55
  1.5 4.9 %collective-permute-start.2 = (f32[2,1,32,128]{3,1,2,0:T(1,128)S(1)}, f32[2,1,32,128]{3,1,2,0:T(1,128)S(1)}, u32[]{:S(2)}, u32[]{:S(2)}) collective-permute-start(f32[2,1,32,128]{3,1,2,0:T(1,128)S(1)} %bitcast.46), channel_id=1, source_target_pairs={{0,8},{8,16},{16,24},{1,9},{9,17},{17,25},{2,10},{10,18},{18,26},{... | collective-permute-start | bytes 98312 | tf_op jit(solution)/shard_map/ppermute | solution.py:14
  6.4 1.1 %fusion.28 = (f32[1,8,32,1]{3,2,1,0:T(8,128)S(1)}, f32[1,8,32,1]{3,2,1,0:T(8,128)S(1)}) fusion(f32[3,8,32,128]{3,2,1,0:T(8,128)} %param.13), kind=kLoop, calls=%fused_computation.70 | loop fusion | bytes 4096 | tf_op jit(solution)/shard_map/slice | solution.py:56
  7.5 0.0 copy-start.8
  7.5 0.1 copy.83
  7.6 0.1 copy.84
  7.7 0.2 copy.67
  8.0 3.4 %collective-permute-start = (f32[2,8,32,1]{3,1,2,0:T(8,128)S(1)}, f32[2,8,32,1]{3,1,2,0:T(8,128)S(1)}, u32[]{:S(2)}, u32[]{:S(2)}) collective-permute-start(f32[2,8,32,1]{3,1,2,0:T(8,128)S(1)} %copy.67), channel_id=1, source_target_pairs={{0,4},{1,5},{2,6},{3,7},{8,12},{9,13},{10,14},{11,15},{16,20},{17,... | collective-permute-start | bytes 6152 | tf_op jit(solution)/shard_map/ppermute | solution.py:14
  11.4 1.2 %copy.64 = f32[3,8,32,128]{3,1,2,0:T(8,128)S(1)} copy(f32[3,8,32,128]{3,2,1,0:T(8,128)} %param.13) | data formatting | bytes 786432 | tf_op args[1]
  12.6 1.3 %collective-permute-start.1 = (f32[2,8,1,128]{3,1,2,0:T(8,128)S(1)}, f32[2,8,1,128]{3,1,2,0:T(8,128)S(1)}, u32[]{:S(2)}, u32[]{:S(2)}) collective-permute-start(f32[2,8,1,128]{3,1,2,0:T(8,128)S(1)} %slice.180), channel_id=1, source_target_pairs={{0,1},{1,2},{2,3},{4,5},{5,6},{6,7},{8,9},{9,10},{10,11},{12,13},{... | collective-permute-start | bytes 24584 | tf_op jit(solution)/shard_map/ppermute | solution.py:14
  14.0 0.0 copy-done.13
  14.0 0.0 copy-done.14
  14.1 0.0 copy-done.7
  14.1 0.7 fusion.31
  14.8 0.1 pad_maximum_fusion.2
  14.9 0.1 mul.80
  15.0 0.1 mul.81
  15.1 0.0 copy-done.8
  15.1 0.1 copy.63
  15.2 0.0 copy-done.9
  15.2 0.1 copy.75
  15.3 1.4 %collective-permute-done = f32[2,8,32,1]{3,1,2,0:T(8,128)S(1)} collective-permute-done((f32[2,8,32,1]{3,1,2,0:T(8,128)S(1)}, f32[2,8,32,1]{3,1,2,0:T(8,128)S(1)}, u32[]{:S(2)}, u32[]{:S(2)}) %collective-permute-start) | collective-permute-done | bytes 2080 | tf_op jit(solution)/shard_map/ppermute | solution.py:14
  16.7 0.0 collective-permute-done.1
  16.7 0.0 collective-permute-done.2
  16.7 0.2 fusion.5
  16.9 0.0 copy-done.3
  16.9 0.0 copy-done.4
  16.9 0.0 copy-start.6
  16.9 0.0 copy-start.10
  16.9 0.0 copy-start.5
  16.9 0.5 fusion.4
  17.5 0.0 copy-start.15
  17.5 0.0 copy-start.1
  17.5 0.7 slice_bitcast_fusion.9
  18.2 0.7 slice_bitcast_fusion.4
  18.9 0.1 slice_bitcast_fusion
  19.0 0.0 copy-done.6
  19.0 0.0 copy-done.10
  19.1 0.3 convolution_multiply_fusion.1
  19.3 0.0 copy-done.5
  19.3 0.4 fusion.1
  19.7 0.0 copy-done.11
  19.7 0.8 %fusion.11 = f32[32,16]{1,0:T(8,128)} fusion(s32[4]{0:T(128)S(1)} %copy-done.15, f32[16]{0:T(128)S(1)} %pad_maximum_fusion.2, f32[4]{0:T(128)S(1)} %fusion.1), kind=kOutput, calls=%fused_computation.48 | convolution fusion | flops 24768 | bytes 2144 | tf_op jit(solution)/shard_map/dot_general | solution.py:99
  20.5 41.7 %all-reduce = f32[32,16]{1,0:T(8,128)S(1)} all-reduce(f32[32,16]{1,0:T(8,128)} %fusion.11), channel_id=2, replica_groups=mesh['gx'=4,'gy'=2,'gz'=4] {'gx','gy','gz'}, use_global_device_ids=true, to_apply=%region_2.0.clone | all-reduce | flops 512 | bytes 4096
  62.3 1.3 %collective-permute-start.3 = (f32[2,8,32,1]{3,1,2,0:T(8,128)S(1)}, f32[2,8,32,1]{3,1,2,0:T(8,128)S(1)}, u32[]{:S(2)}, u32[]{:S(2)}) collective-permute-start(f32[2,8,32,1]{3,1,2,0:T(8,128)S(1)} %pad_maximum_fusion), channel_id=1, source_target_pairs={{4,0},{5,1},{6,2},{7,3},{12,8},{13,9},{14,10},{15,11},{20,16},{21,... | collective-permute-start | bytes 6152 | tf_op jit(solution)/shard_map/ppermute | solution.py:14
  63.6 0.9 %slice_bitcast_fusion.5 = f32[1,8,31,128]{3,1,2,0:T(8,128)S(1)} fusion(f32[8,32,128]{2,0,1:T(8,128)} %get-tuple-element.21), kind=kLoop, calls=%fused_computation.35 | loop fusion | bytes 253952 | tf_op jit(solution)/shard_map/concatenate | solution.py:25
  64.5 0.1 slice_bitcast_fusion.1
  64.6 0.0 copy-start.12
  64.6 0.0 copy-start.2
  64.6 2.5 %multiply_add_fusion = f32[16,8,32,128]{3,2,1,0:T(8,128)} fusion(f32[16,8,32,128]{3,2,1,0:T(8,128)S(1)} %copy-done.1, f32[8,32,128]{2,1,0:T(8,128)S(1)} %copy.78, f32[16]{0:T(128)} %copy-done.11), kind=kLoop, calls=%fused_computation | loop fusion | flops 1048576 | bytes 4325440 | tf_op jit(solution)/shard_map/add | solution.py:85
  67.1 0.0 copy-done.12
  67.1 0.5 dynamic-slice_add_fusion
  67.6 0.8 %copy.81 = f32[3,8,32,128]{3,2,1,0:T(8,128)} copy(f32[3,8,32,128]{3,1,2,0:T(8,128)S(1)} %get-tuple-element.17) | data formatting | bytes 786432
  68.5 1.3 %collective-permute-start.4 = (f32[2,8,1,128]{3,1,2,0:T(8,128)S(1)}, f32[2,8,1,128]{3,1,2,0:T(8,128)S(1)}, u32[]{:S(2)}, u32[]{:S(2)}) collective-permute-start(f32[2,8,1,128]{3,1,2,0:T(8,128)S(1)} %slice.199), channel_id=1, source_target_pairs={{1,0},{2,1},{3,2},{5,4},{6,5},{7,6},{9,8},{10,9},{11,10},{13,12},{... | collective-permute-start | bytes 24584 | tf_op jit(solution)/shard_map/ppermute | solution.py:14
  69.8 1.3 %collective-permute-start.5 = (f32[2,1,32,128]{3,1,2,0:T(1,128)S(1)}, f32[2,1,32,128]{3,1,2,0:T(1,128)S(1)}, u32[]{:S(2)}, u32[]{:S(2)}) collective-permute-start(f32[2,1,32,128]{3,1,2,0:T(1,128)S(1)} %slice.205), channel_id=1, source_target_pairs={{8,0},{16,8},{24,16},{9,1},{17,9},{25,17},{10,2},{18,10},{26,18},{... | collective-permute-start | bytes 98312 | tf_op jit(solution)/shard_map/ppermute | solution.py:14
  71.1 0.3 collective-permute-done.3
  71.4 0.1 collective-permute-done.4
  71.5 4.2 %collective-permute-done.5 = f32[2,1,32,128]{3,1,2,0:T(1,128)S(1)} collective-permute-done((f32[2,1,32,128]{3,1,2,0:T(1,128)S(1)}, f32[2,1,32,128]{3,1,2,0:T(1,128)S(1)}, u32[]{:S(2)}, u32[]{:S(2)}) %collective-permute-start.5) | collective-permute-done | bytes 32800 | tf_op jit(solution)/shard_map/ppermute | solution.py:14
  75.8 0.2 fusion.8
  76.0 0.3 fusion.3
  76.2 0.8 %copy.82 = f32[3,8,32,128]{3,2,1,0:T(8,128)} copy(f32[3,8,32,128]{3,1,2,0:T(8,128)S(1)} %fusion.3) | data formatting | bytes 786432
  (31 shorter events, 0.3 us)
Async XLA Ops:
  0.6 13.4 %copy-start.13 = (s32[1,1,16]{2,1,0:T(1,128)S(1)}, s32[1,1,16]{2,1,0:T(1,128)}, u32[]{:S(2)}) copy-start(s32[1,1,16]{2,1,0:T(1,128)} %param.18) | copy-start | bytes 196
  0.6 13.4 %copy-start.14 = (f32[8]{0:T(128)S(1)}, f32[8]{0:T(128)}, u32[]{:S(2)}) copy-start(f32[8]{0:T(128)} %param.19) | copy-start | bytes 100
  0.7 13.4 %copy-start.7 = (f32[4,2,32,128]{3,2,1,0:T(8,128)S(1)}, f32[4,2,32,128]{3,2,1,0:T(8,128)}, u32[]{:S(2)}) copy-start(f32[4,2,32,128]{3,2,1,0:T(8,128)} %param.22) | copy-start | bytes 393220
  1.5 15.2 %collective-permute-start.2 = (f32[2,1,32,128]{3,1,2,0:T(1,128)S(1)}, f32[2,1,32,128]{3,1,2,0:T(1,128)S(1)}, u32[]{:S(2)}, u32[]{:S(2)}) collective-permute-start(f32[2,1,32,128]{3,1,2,0:T(1,128)S(1)} %bitcast.46), channel_id=1, source_target_pairs={{0,8},{8,16},{16,24},{1,9},{9,17},{17,25},{2,10},{10,18},{18,26},{... | collective-permute-start | bytes 98312 | tf_op jit(solution)/shard_map/ppermute | solution.py:14
  7.5 7.6 %copy-start.8 = (f32[8,32,128]{2,1,0:T(8,128)S(1)}, f32[8,32,128]{2,1,0:T(8,128)}, u32[]{:S(2)}) copy-start(f32[8,32,128]{2,1,0:T(8,128)} %param.15) | copy-start | bytes 393220
  7.6 7.5 %copy-start.9 = (f32[8,32,128]{2,1,0:T(8,128)S(1)}, f32[8,32,128]{2,1,0:T(8,128)}, u32[]{:S(2)}) copy-start(f32[8,32,128]{2,1,0:T(8,128)} %param.16) | copy-start | bytes 393220
  8.0 8.7 %collective-permute-start = (f32[2,8,32,1]{3,1,2,0:T(8,128)S(1)}, f32[2,8,32,1]{3,1,2,0:T(8,128)S(1)}, u32[]{:S(2)}, u32[]{:S(2)}) collective-permute-start(f32[2,8,32,1]{3,1,2,0:T(8,128)S(1)} %copy.67), channel_id=1, source_target_pairs={{0,4},{1,5},{2,6},{3,7},{8,12},{9,13},{10,14},{11,15},{16,20},{17,... | collective-permute-start | bytes 6152 | tf_op jit(solution)/shard_map/ppermute | solution.py:14
  12.6 4.0 %collective-permute-start.1 = (f32[2,8,1,128]{3,1,2,0:T(8,128)S(1)}, f32[2,8,1,128]{3,1,2,0:T(8,128)S(1)}, u32[]{:S(2)}, u32[]{:S(2)}) collective-permute-start(f32[2,8,1,128]{3,1,2,0:T(8,128)S(1)} %slice.180), channel_id=1, source_target_pairs={{0,1},{1,2},{2,3},{4,5},{5,6},{6,7},{8,9},{9,10},{10,11},{12,13},{... | collective-permute-start | bytes 24584 | tf_op jit(solution)/shard_map/ppermute | solution.py:14
  14.8 2.1 %copy-start.3 = (f32[3,8,32,128]{3,2,1,0:T(8,128)S(1)}, f32[3,8,32,128]{3,2,1,0:T(8,128)}, u32[]{:S(2)}) copy-start(f32[3,8,32,128]{3,2,1,0:T(8,128)} %param.14) | copy-start | bytes 1179652
  14.8 2.1 %copy-start.4 = (f32[3,8,32,128]{3,2,1,0:T(8,128)S(1)}, f32[3,8,32,128]{3,2,1,0:T(8,128)}, u32[]{:S(2)}) copy-start(f32[3,8,32,128]{3,2,1,0:T(8,128)} %param.12) | copy-start | bytes 1179652
  14.9 4.8 %copy-start.11 = (f32[16]{0:T(128)}, f32[16]{0:T(128)S(1)}, u32[]{:S(2)}) copy-start(f32[16]{0:T(128)S(1)} %pad_maximum_fusion.2) | copy-start | bytes 196
  16.9 2.1 %copy-start.6 = (f32[4,1,32,128]{3,2,1,0:T(8,128)S(1)}, f32[4,1,32,128]{3,2,1,0:T(8,128)}, u32[]{:S(2)}) copy-start(f32[4,1,32,128]{3,2,1,0:T(8,128)} %get-tuple-element.43) | copy-start | bytes 196612
  16.9 2.1 %copy-start.10 = (s32[4]{0:T(128)S(1)}, s32[4]{0:T(128)}, u32[]{:S(2)}) copy-start(s32[4]{0:T(128)} %param.20) | copy-start | bytes 52
  16.9 2.4 %copy-start.5 = (f32[4,1,32,128]{3,2,1,0:T(8,128)S(1)}, f32[4,1,32,128]{3,2,1,0:T(8,128)}, u32[]{:S(2)}) copy-start(f32[4,1,32,128]{3,2,1,0:T(8,128)} %get-tuple-element.42) | copy-start | bytes 196612
  17.5 2.3 %copy-start.15 = (s32[4]{0:T(128)S(1)}, s32[4]{0:T(128)}, u32[]{:S(2)}) copy-start(s32[4]{0:T(128)} %param.21) | copy-start | bytes 52
  17.5 47.1 %copy-start.1 = (f32[16,8,32,128]{3,2,1,0:T(8,128)S(1)}, f32[16,8,32,128]{3,2,1,0:T(8,128)}, u32[]{:S(2)}) copy-start(f32[16,8,32,128]{3,2,1,0:T(8,128)} %param.17) | copy-start | bytes 6291460
  62.3 9.1 %collective-permute-start.3 = (f32[2,8,32,1]{3,1,2,0:T(8,128)S(1)}, f32[2,8,32,1]{3,1,2,0:T(8,128)S(1)}, u32[]{:S(2)}, u32[]{:S(2)}) collective-permute-start(f32[2,8,32,1]{3,1,2,0:T(8,128)S(1)} %pad_maximum_fusion), channel_id=1, source_target_pairs={{4,0},{5,1},{6,2},{7,3},{12,8},{13,9},{14,10},{15,11},{20,16},{21,... | collective-permute-start | bytes 6152 | tf_op jit(solution)/shard_map/ppermute | solution.py:14
  64.6 2.5 %copy-start.12 = (f32[1,16]{1,0:T(1,128)S(1)}, f32[1,16]{1,0:T(1,128)}, u32[]{:S(2)}) copy-start(f32[1,16]{1,0:T(1,128)} %param.23) | copy-start | bytes 196
  64.6 11.2 %copy-start.2 = (f32[1,8,31,128]{3,1,2,0:T(8,128)S(1)}, f32[1,8,31,128]{3,1,2,0:T(8,128)}, u32[]{:S(2)}) copy-start(f32[1,8,31,128]{3,1,2,0:T(8,128)} %slice_bitcast_fusion.4) | copy-start | bytes 380932
  67.1 8.8 %copy-start = (f32[3,8,32,128]{3,2,1,0:T(8,128)S(1)}, f32[3,8,32,128]{3,2,1,0:T(8,128)}, u32[]{:S(2)}) copy-start(f32[3,8,32,128]{3,2,1,0:T(8,128)} %param.13) | copy-start | bytes 1179652
  68.5 3.1 %collective-permute-start.4 = (f32[2,8,1,128]{3,1,2,0:T(8,128)S(1)}, f32[2,8,1,128]{3,1,2,0:T(8,128)S(1)}, u32[]{:S(2)}, u32[]{:S(2)}) collective-permute-start(f32[2,8,1,128]{3,1,2,0:T(8,128)S(1)} %slice.199), channel_id=1, source_target_pairs={{1,0},{2,1},{3,2},{5,4},{6,5},{7,6},{9,8},{10,9},{11,10},{13,12},{... | collective-permute-start | bytes 24584 | tf_op jit(solution)/shard_map/ppermute | solution.py:14
  69.8 6.0 %collective-permute-start.5 = (f32[2,1,32,128]{3,1,2,0:T(1,128)S(1)}, f32[2,1,32,128]{3,1,2,0:T(1,128)S(1)}, u32[]{:S(2)}, u32[]{:S(2)}) collective-permute-start(f32[2,1,32,128]{3,1,2,0:T(1,128)S(1)} %slice.205), channel_id=1, source_target_pairs={{8,0},{16,8},{24,16},{9,1},{17,9},{25,17},{10,2},{18,10},{26,18},{... | collective-permute-start | bytes 98312 | tf_op jit(solution)/shard_map/ppermute | solution.py:14
where the time goes:
time: 78.4 us; the launch traced here: 77 us
  blocking collectives  41.7 us (53%)
  starting transfers between devices  13.5 us (17%)
  local copies, waits for them, and re-layouts  8.91 us (11%)
  waiting for transfers between devices  6.07 us (8%)
  other arithmetic  4.31 us (5%)
  matrix products  1.46 us (2%)
  between operations  1.1 us (1%)
    unnamed x1, blocking collectives  41.7 us
    ppermute x6, starting transfers between devices, from_behind(): return lax.ppermute(x, axis, pairs)  13.5 us
    ppermute x6, waiting for transfers between devices, from_behind(): return lax.ppermute(x, axis, pairs)  6.07 us
    unnamed x39, local copies, waits for them, and re-layouts  3.33 us
    add x1, other arithmetic, body(): dft_next = dft_acc + phase[:, None, None, None] * product[None]  2.5 us
    concatenate x4, local copies, waits for them, and re-layouts, upper_diff(): jnp.concatenate([lax.slice_in_dim(field, 1, size, axis=along), above], al...  1.75 us
  transfers between devices with their start and end apart: 6, of which 4 were waited for; matrix products, arithmetic and copies ran while one was open for 11% of the time, Pallas kernels for 0%

commit v1 on v0

v1 whole, which is shorter than its diff:
```python
import functools

import jax
import jax.numpy as jnp
from jax import lax
from jax.experimental import pallas as pl
from jax.experimental.pallas import tpu as pltpu
from jax.sharding import PartitionSpec as P

BY = 8
NF = 8
NP = 4
UNROLL = 32


def tiles(plane):
    return [plane[8 * q : 8 * q + 8] for q in range(plane.shape[0] // 8)]


def pack_lane(fields, lane_of, lane):
    packed = jnp.zeros((8, 128), jnp.float32)
    k = 0
    for plane in fields:
        for tile in tiles(plane):
            moved = pltpu.roll(tile, (k - lane_of) % 128, 1)
            packed = jnp.where(lane == k, moved, packed)
            k += 1
    return packed


def unpack_lane(packed, first, count, lane_of, keep):
    out = [pltpu.roll(packed, (lane_of - first - q) % 128, 1) for q in range(count)]
    return jnp.where(keep, jnp.concatenate(out, 0), 0.0)


def step(
    sizes, e_hbm, h_hbm, ef_hbm, ec_hbm, hc_hbm, dft_hbm, modes_hbm,
    mask_ref, omega_ref, pidx_ref, powner_ref, mon_ref,
    en, hn, dn, mon_out,
    ef, ec, hc, modes,
    hx_in, hy_in, hz_in, ex_in, ey_in, ez_in, hy_out, ey_out, mine, rows,
    load_sems, h_send, h_recv, e_send, e_recv, all_send, all_recv,
):
    n_gx, n_gy, n_gz = sizes
    n = n_gx * n_gy * n_gz
    a, b, c = lax.axis_index("gx"), lax.axis_index("gy"), lax.axis_index("gz")
    stride_x, stride_y = n_gy * n_gz, n_gz
    me = a * stride_x + b * stride_y + c
    nx, nz, ny = ec.shape
    zt = nz // 8

    def each_other(run):
        if n <= UNROLL:
            for k in range(1, n):
                run(k, lax.rem(me + k, n))
        else:
            lax.fori_loop(1, n, lambda k, _: (run(k, lax.rem(me + k, n)), 0)[1], 0)

    barrier = pltpu.get_barrier_semaphore()
    loads = [
        pltpu.make_async_copy(src, dst, load_sems.at[i])
        for i, (src, dst) in enumerate(
            [(h_hbm, hn), (e_hbm, en), (ec_hbm, ec), (modes_hbm, modes), (hc_hbm, hc), (ef_hbm, ef), (dft_hbm, dn)]
        )
    ]
    for load in loads[:3]:
        load.start()
    each_other(
        lambda k, dev: pl.semaphore_signal(
            barrier, inc=1, device_id=dev, device_id_type=pl.DeviceIdType.LOGICAL
        )
    )
    for load in loads[3:]:
        load.start()

    def remote(src, dst, send, recv, dev):
        return pltpu.make_async_remote_copy(
            src_ref=src, dst_ref=dst, send_sem=send, recv_sem=recv,
            device_id=dev, device_id_type=pl.DeviceIdType.LOGICAL,
        )

    up = [(a < n_gx - 1, stride_x), (b < n_gy - 1, stride_y), (c < n_gz - 1, 1)]
    down = [(a > 0, stride_x), (b > 0, stride_y), (c > 0, 1)]
    h_copies = [
        remote(src, dst, h_send.at[i], h_recv.at[i], jnp.where(up[i][0], me + up[i][1], 0))
        for i, (src, dst) in enumerate(
            [(hn.at[1:3, nx - 1], hx_in), (hy_out, hy_in), (hn.at[0:2, :, nz - 1], hz_in)]
        )
    ]
    e_copies = [
        remote(src, dst, e_send.at[i], e_recv.at[i], jnp.where(down[i][0], me - down[i][1], 0))
        for i, (src, dst) in enumerate(
            [(en.at[1:3, 0], ex_in), (ey_out, ey_in), (en.at[0:2, :, 0], ez_in)]
        )
    ]

    row = lax.broadcasted_iota(jnp.int32, (nz, ny), 0)
    lane = lax.broadcasted_iota(jnp.int32, (nz, ny), 1)
    lane8 = lax.broadcasted_iota(jnp.int32, (8, 128), 1)

    loads[0].wait()
    hy_out[...] = pack_lane(
        [hn[comp, x] for comp in (0, 2) for x in range(nx)], ny - 1, lane8
    )
    pl.semaphore_wait(barrier, n - 1)
    for i in (0, 2, 1):
        pl.when(up[i][0])(h_copies[i].start)

    sub8 = lax.broadcasted_iota(jnp.int32, (8, 128), 0)
    angle_rows = jnp.zeros((8, 128), jnp.float32)
    angle_lanes = jnp.zeros((8, 128), jnp.float32)
    for f in range(NF):
        angle_rows = jnp.where(sub8 == f, omega_ref[f], angle_rows)
        angle_lanes = jnp.where((lane8 == f) | (lane8 == f + NF), omega_ref[f], angle_lanes)
    cosines, sines = jnp.cos(angle_rows), -jnp.sin(angle_rows)
    phase_lanes = jnp.where(lane8 < NF, jnp.cos(angle_lanes), -jnp.sin(angle_lanes))
    weight = jnp.zeros((8, 128), jnp.float32)
    for k in range(ny // BY):
        weight = jnp.where(lane8 // BY == k, mask_ref[0, 0, k].astype(jnp.float32), weight)
    weight = jnp.concatenate([weight] * zt, 0)

    loads[1].wait()
    loads[2].wait()

    def low(plane, axis):
        first = (row if axis == 0 else lane) == 0
        return plane - jnp.where(first, 0.0, pltpu.roll(plane, 1, axis))

    for x in range(nx):
        h0, h1, h2 = hn[0, x], hn[1, x], hn[2, x]
        d1 = h1 - hn[1, x - 1] if x else h1
        d2 = h2 - hn[2, x - 1] if x else h2
        coef = ec[x]
        en[0, x] = en[0, x] - coef * (low(h2, 1) - low(h1, 0))
        en[1, x] = en[1, x] - coef * (low(h0, 0) - d2)
        en[2, x] = en[2, x] - coef * (d1 - low(h0, 1))

    for i, landing in enumerate((hx_in, hy_in, hz_in)):
        pl.when(down[i][0])(h_copies[i].wait_recv)

        @pl.when(jnp.logical_not(down[i][0]))
        def _(landing=landing):
            landing[...] = jnp.zeros_like(landing)

    packed = hy_in[...]
    for x in range(nx):
        coef = ec[x]
        y0 = unpack_lane(packed, x * zt, zt, 0, lane == 0)
        y2 = unpack_lane(packed, (nx + x) * zt, zt, 0, lane == 0)
        z0 = jnp.where(sub8 == 0, hz_in[0, x : x + 1, :], 0.0)
        z1 = jnp.where(sub8 == 0, hz_in[1, x : x + 1, :], 0.0)
        rest = jnp.zeros((nz - 8, ny), jnp.float32)
        z0, z1 = jnp.concatenate([z0, rest], 0), jnp.concatenate([z1, rest], 0)
        add0, add1, add2 = y2 - z1, z0, -y0
        if x == 0:
            add1 = add1 - hx_in[1]
            add2 = add2 + hx_in[0]
        en[0, x] = en[0, x] + coef * add0
        en[1, x] = en[1, x] + coef * add1
        en[2, x] = en[2, x] + coef * add2

    loads[3].wait()
    share = jnp.zeros((8, 128), jnp.float32)
    for p in range(NP):
        x_of = pidx_ref[p] - a * nx
        inside = (x_of >= 0) & (x_of < nx)
        at = jnp.clip(x_of, 0, nx - 1)
        both = modes[p, 0] * en[1, at] + modes[p, 1] * en[2, at]
        total = functools.reduce(jnp.add, tiles(both))
        total = jnp.sum(jnp.sum(total, axis=0, keepdims=True), axis=1, keepdims=True)
        total = jnp.where(inside, total, 0.0)
        share = jnp.where(lane8 == p, total, share)
    mine[...] = share[0:1]

    def send_row(k, dev):
        remote(mine, rows.at[k - 1], all_send, all_recv, dev).start()

    each_other(send_row)
    for i in (0, 2):
        pl.when(down[i][0])(e_copies[i].start)
    ey_out[...] = pack_lane([en[comp, x] for comp in (0, 2) for x in range(nx)], 0, lane8)
    pl.when(down[1][0])(e_copies[1].start)

    for i in range(3):
        pl.when(up[i][0])(h_copies[i].wait_send)
    loads[4].wait()

    def high(plane, axis):
        last = (row == nz - 1) if axis == 0 else (lane == ny - 1)
        return jnp.where(last, 0.0, pltpu.roll(plane, plane.shape[axis] - 1, axis)) - plane

    for x in range(nx):
        e0, e1, e2 = en[0, x], en[1, x], en[2, x]
        d1 = en[1, x + 1] - e1 if x < nx - 1 else -e1
        d2 = en[2, x + 1] - e2 if x < nx - 1 else -e2
        coef = hc[x]
        hn[0, x] = hn[0, x] + coef * (high(e2, 1) - high(e1, 0))
        hn[1, x] = hn[1, x] + coef * (high(e0, 0) - d2)
        hn[2, x] = hn[2, x] + coef * (d1 - high(e0, 1))

    loads[5].wait()
    loads[6].wait()
    for x in range(nx):
        product = weight * (ef[0, x] * en[0, x] + ef[1, x] * en[1, x] + ef[2, x] * en[2, x])
        for f in range(NF):
            dn[f, x] = dn[f, x] + cosines[f : f + 1] * product
            dn[NF + f, x] = dn[NF + f, x] + sines[f : f + 1] * product

    for i, landing in enumerate((ex_in, ey_in, ez_in)):
        pl.when(up[i][0])(e_copies[i].wait_recv)

        @pl.when(jnp.logical_not(up[i][0]))
        def _(landing=landing):
            landing[...] = jnp.zeros_like(landing)

    packed = ey_in[...]
    for x in range(nx):
        coef = hc[x]
        y0 = unpack_lane(packed, x * zt, zt, ny - 1, lane == ny - 1)
        y2 = unpack_lane(packed, (nx + x) * zt, zt, ny - 1, lane == ny - 1)
        z0 = jnp.where(sub8 == 7, ez_in[0, x : x + 1, :], 0.0)
        z1 = jnp.where(sub8 == 7, ez_in[1, x : x + 1, :], 0.0)
        rest = jnp.zeros((nz - 8, ny), jnp.float32)
        z0, z1 = jnp.concatenate([rest, z0], 0), jnp.concatenate([rest, z1], 0)
        add0, add1, add2 = y2 - z1, z0, -y0
        if x == nx - 1:
            add1 = add1 - ex_in[1]
            add2 = add2 + ex_in[0]
        hn[0, x] = hn[0, x] + coef * add0
        hn[1, x] = hn[1, x] + coef * add1
        hn[2, x] = hn[2, x] + coef * add2
    for i in range(3):
        pl.when(down[i][0])(e_copies[i].wait_send)

    remote(rows, rows, all_send, all_recv, me).wait()
    intersection = jnp.sum(rows[...], axis=0) + mine[...]
    lane1 = lax.broadcasted_iota(jnp.int32, (1, 128), 1)
    owned = jnp.zeros((1, 128), jnp.float32)
    for p in range(NP):
        owned = jnp.where(lane1 == p, (powner_ref[p] == me).astype(jnp.float32), owned)
    total = jnp.sum(owned * intersection, axis=1, keepdims=True)
    mon_out[...] = mon_ref[...] + total * phase_lanes[0:1, : 2 * NF]


def write_out(en, hn, dn, mon, en_out, hn_out, dn_out, mon_out, sems):
    parts = 4
    size = dn.shape[0] // parts
    pairs = [(dn.at[pl.ds(i * size, size)], dn_out.at[pl.ds(i * size, size)]) for i in range(parts)]
    pairs += [(en, en_out), (hn, hn_out), (mon, mon_out)]
    copies = [pltpu.make_async_copy(src, dst, sems.at[i]) for i, (src, dst) in enumerate(pairs)]
    for copy in copies:
        copy.start()
    for copy in copies:
        copy.wait()


def body(sizes, e_field, h_field, e_forward, e_coeff, h_coeff, dft_acc, design_mask,
         omega_t, port_index, port_owner, port_modes, monitor_acc):
    n = sizes[0] * sizes[1] * sizes[2]
    nx, nz, ny = e_coeff.shape
    f32 = jnp.float32
    hbm = pl.BlockSpec(memory_space=pltpu.HBM)
    vmem = pl.BlockSpec(memory_space=pltpu.VMEM)
    smem = pl.BlockSpec(memory_space=pltpu.SMEM)
    held = pl.pallas_call(
        functools.partial(step, sizes),
        out_shape=[
            pltpu.VMEM(e_field.shape, f32),
            pltpu.VMEM(h_field.shape, f32),
            pltpu.VMEM(dft_acc.shape, f32),
            pltpu.VMEM(monitor_acc.shape, f32),
        ],
        in_specs=[hbm] * 7 + [smem] * 4 + [vmem],
        out_specs=[vmem] * 4,
        scratch_shapes=[
            pltpu.VMEM(e_forward.shape, f32),
            pltpu.VMEM(e_coeff.shape, f32),
            pltpu.VMEM(h_coeff.shape, f32),
            pltpu.VMEM(port_modes.shape, f32),
            pltpu.VMEM((2, nz, ny), f32),
            pltpu.VMEM((8, 128), f32),
            pltpu.VMEM((2, nx, ny), f32),
            pltpu.VMEM((2, nz, ny), f32),
            pltpu.VMEM((8, 128), f32),
            pltpu.VMEM((2, nx, ny), f32),
            pltpu.VMEM((8, 128), f32),
            pltpu.VMEM((8, 128), f32),
            pltpu.VMEM((1, 128), f32),
            pltpu.VMEM((n - 1, 1, 128), f32),
            pltpu.SemaphoreType.DMA((7,)),
            pltpu.SemaphoreType.DMA((3,)),
            pltpu.SemaphoreType.DMA((3,)),
            pltpu.SemaphoreType.DMA((3,)),
            pltpu.SemaphoreType.DMA((3,)),
            pltpu.SemaphoreType.DMA,
            pltpu.SemaphoreType.DMA,
        ],
        compiler_params=pltpu.CompilerParams(
            collective_id=0, has_side_effects=True, vmem_limit_bytes=24 * 2**20
        ),
        name="yee_step",
    )(e_field, h_field, e_forward, e_coeff, h_coeff, dft_acc, port_modes,
      design_mask, omega_t, port_index, port_owner, monitor_acc)
    shape = lambda x: jax.ShapeDtypeStruct(x.shape, f32)
    return pl.pallas_call(
        write_out,
        out_shape=[shape(x) for x in (e_field, h_field, dft_acc, monitor_acc)],
        in_specs=[vmem] * 4,
        out_specs=[hbm] * 4,
        scratch_shapes=[pltpu.SemaphoreType.DMA((7,))],
        name="write_out",
    )(*held)


def solution(mesh):
    grid = P(None, "gx", "gz", "gy")
    brick = P("gx", "gz", "gy")
    own = P(("gx", "gy", "gz"), None)
    sizes = tuple(mesh.shape[axis] for axis in ("gx", "gy", "gz"))
    in_specs = (grid, grid, grid, brick, brick, grid, brick, P(), P(), P(),
                P(None, None, "gz", "gy"), own)
    return jax.shard_map(
        functools.partial(body, sizes), mesh=mesh, in_specs=in_specs,
        out_specs=(grid, grid, grid, own), check_vma=False,
    )
```

time: 78.4 us -> 33.2 us (0.42); the launches traced: 77 us -> 32.8 us
  blocking collectives: 41.7 us -> 0 us
  Pallas kernels: 0 us -> 18.2 us
  starting transfers between devices: 13.5 us -> 0 us
  waiting for transfers between devices: 6.07 us -> 0 us
  local copies, waits for them, and re-layouts: 8.91 us -> 13.9 us
  other arithmetic: 4.31 us -> 0 us
  matrix products: 1.46 us -> 0 us
    unnamed x1 -> x0, blocking collectives: 41.7 us -> none
    pallas_call x0 -> x2, Pallas kernels: none -> 18.2 us  [the longest x1 14.7 us: body(): pl.pallas_call(functools.partial(step, sizes), out_shape=[pltpu.VMEM(e_fi...]
    ppermute x6 -> x0, starting transfers between devices: 13.5 us -> none  [from_behind(): return lax.ppermute(x, axis, pairs)]
    unnamed x39 -> x32, local copies, waits for them, and re-layouts: 3.33 us -> 13.9 us
    ppermute x6 -> x0, waiting for transfers between devices: 6.07 us -> none  [from_behind(): return lax.ppermute(x, axis, pairs)]
    add x4 -> x0, other arithmetic: 3.28 us -> none  [the longest x1 2.5 us: body(): dft_next = dft_acc + phase[:, None, None, None] * product[None]]
    slice x15 -> x0, local copies, waits for them, and re-layouts: 2.69 us -> none  [the longest x1 1.09 us: body(): h_field[0, :, :, -1:]]
    concatenate x6 -> x0, local copies, waits for them, and re-layouts: 1.79 us -> none  [the longest x4 1.75 us: upper_diff(): jnp.concatenate([lax.slice_in_dim(field, 1, size, axis=along), above], al...]
  transfers between devices with their start and end apart: 6 -> 0, of which waited for: 4 -> 0; matrix products, arithmetic and copies ran while one was open for 11% -> 0% of each run, Pallas kernels for 0% -> 0%
where the time goes in v1:
time: 33.2 us; the launch traced here: 32.8 us
  Pallas kernels  18.2 us (55%)
  local copies, waits for them, and re-layouts  13.9 us (42%)
  between operations  0.68 us (2%)
    pallas_call x1, Pallas kernels, body(): pl.pallas_call(functools.partial(step, sizes), out_shape=[pltpu.VMEM(e_fi...  14.7 us
    unnamed x32, local copies, waits for them, and re-layouts  13.9 us
    pallas_call x1, Pallas kernels, body(): pl.pallas_call(write_out, out_shape=[shape(x) for x in (e_field, h_field,...  3.48 us

profile of v1, /device:TPU:0, one launch (start us, length us, event | category | flops | bytes accessed | tf_op | source)
XLA Modules:
  0.0 32.8 jit_solution(4565963921500165336)
XLA Ops:
  0.6 0.0 copy-start
  0.6 1.6 %copy-done = f32[16,8,32,128]{3,2,1,0:T(8,128)S(1)} copy-done((f32[16,8,32,128]{3,2,1,0:T(8,128)S(1)}, f32[16,8,32,128]{3,2,1,0:T(8,128)}, u32[]{:S(2)}) %copy-start) | copy-done | bytes 2097176
  2.2 0.0 copy-start.2
  2.2 1.0 %copy-done.2 = f32[3,8,32,128]{3,2,1,0:T(8,128)S(1)} copy-done((f32[3,8,32,128]{3,2,1,0:T(8,128)S(1)}, f32[3,8,32,128]{3,2,1,0:T(8,128)}, u32[]{:S(2)}) %copy-start.2) | copy-done | bytes 393240
  3.2 0.0 copy-start.3
  3.2 1.0 %copy-done.3 = f32[3,8,32,128]{3,2,1,0:T(8,128)S(1)} copy-done((f32[3,8,32,128]{3,2,1,0:T(8,128)S(1)}, f32[3,8,32,128]{3,2,1,0:T(8,128)}, u32[]{:S(2)}) %copy-start.3) | copy-done | bytes 393240
  4.2 0.0 copy-start.4
  4.2 1.0 %copy-done.4 = f32[3,8,32,128]{3,2,1,0:T(8,128)S(1)} copy-done((f32[3,8,32,128]{3,2,1,0:T(8,128)S(1)}, f32[3,8,32,128]{3,2,1,0:T(8,128)}, u32[]{:S(2)}) %copy-start.4) | copy-done | bytes 393240
  5.2 0.0 copy-start.7
  5.2 0.9 %copy-done.7 = f32[8,32,128]{2,1,0:T(8,128)S(1)} copy-done((f32[8,32,128]{2,1,0:T(8,128)S(1)}, f32[8,32,128]{2,1,0:T(8,128)}, u32[]{:S(2)}) %copy-start.7) | copy-done | bytes 131096
  6.1 0.0 copy-start.8
  6.1 0.9 %copy-done.8 = f32[8,32,128]{2,1,0:T(8,128)S(1)} copy-done((f32[8,32,128]{2,1,0:T(8,128)S(1)}, f32[8,32,128]{2,1,0:T(8,128)}, u32[]{:S(2)}) %copy-start.8) | copy-done | bytes 131096
  7.0 0.0 copy-start.9
  7.0 0.9 %copy-done.9 = f32[4,2,32,128]{3,2,1,0:T(8,128)S(1)} copy-done((f32[4,2,32,128]{3,2,1,0:T(8,128)S(1)}, f32[4,2,32,128]{3,2,1,0:T(8,128)}, u32[]{:S(2)}) %copy-start.9) | copy-done | bytes 131096
  7.9 0.0 copy-start.10
  7.9 0.7 %copy-done.10 = s32[1,1,16]{2,1,0:T(1,128)S(1)} copy-done((s32[1,1,16]{2,1,0:T(1,128)S(1)}, s32[1,1,16]{2,1,0:T(1,128)}, u32[]{:S(2)}) %copy-start.10) | copy-done | bytes 88
  8.6 0.0 copy-start.11
  8.6 0.7 %copy-done.11 = f32[8]{0:T(128)S(1)} copy-done((f32[8]{0:T(128)S(1)}, f32[8]{0:T(128)}, u32[]{:S(2)}) %copy-start.11) | copy-done | bytes 56
  9.2 0.0 copy-start.12
  9.2 0.7 %copy-done.12 = s32[4]{0:T(128)S(1)} copy-done((s32[4]{0:T(128)S(1)}, s32[4]{0:T(128)}, u32[]{:S(2)}) %copy-start.12) | copy-done | bytes 40
  9.9 0.0 copy-start.13
  9.9 0.7 %copy-done.13 = s32[4]{0:T(128)S(1)} copy-done((s32[4]{0:T(128)S(1)}, s32[4]{0:T(128)}, u32[]{:S(2)}) %copy-start.13) | copy-done | bytes 40
  10.6 0.0 copy-start.14
  10.6 0.7 %copy-done.14 = f32[1,16]{1,0:T(1,128)S(1)} copy-done((f32[1,16]{1,0:T(1,128)S(1)}, f32[1,16]{1,0:T(1,128)}, u32[]{:S(2)}) %copy-start.14) | copy-done | bytes 88
  11.2 14.7 %yee_step.1 = (f32[3,8,32,128]{3,2,1,0:T(8,128)S(1)}, f32[3,8,32,128]{3,2,1,0:T(8,128)S(1)}, f32[16,8,32,128]{3,2,1,0:T(8,128)S(1)}, f32[1,16]{1,0:T(1,128)S(1)}) custom-call(f32[3,8,32,128]{3,2,1,0:T(8,128)S(1)} %copy-done.2, f32[3,8,32,128]{3,2,1,0:T(8,128)S(1)} %copy-done.3, f32[3,8,32,128]{3,2,1,0:T(8,128)S(1)} %copy-done.4, ...), custom_call_target="tpu_custom_call" | custom-call | tf_op jit(solution)/shard_map/yee_step/pallas_call | solution.py:265
  25.9 0.0 copy-start.1
  26.0 1.3 %copy-done.1 = f32[16,8,32,128]{3,2,1,0:T(8,128)} copy-done((f32[16,8,32,128]{3,2,1,0:T(8,128)}, f32[16,8,32,128]{3,2,1,0:T(8,128)S(1)}, u32[]{:S(2)}) %copy-start.1) | copy-done | bytes 2097176
  27.3 0.0 copy-start.5
  27.3 0.7 %copy-done.5 = f32[3,8,32,128]{3,2,1,0:T(8,128)} copy-done((f32[3,8,32,128]{3,2,1,0:T(8,128)}, f32[3,8,32,128]{3,2,1,0:T(8,128)S(1)}, u32[]{:S(2)}) %copy-start.5) | copy-done | bytes 393240
  28.0 0.0 copy-start.6
  28.0 0.8 %copy-done.6 = f32[3,8,32,128]{3,2,1,0:T(8,128)} copy-done((f32[3,8,32,128]{3,2,1,0:T(8,128)}, f32[3,8,32,128]{3,2,1,0:T(8,128)S(1)}, u32[]{:S(2)}) %copy-start.6) | copy-done | bytes 393240
  28.8 0.0 copy-start.15
  28.8 0.5 %copy-done.15 = f32[1,16]{1,0:T(1,128)} copy-done((f32[1,16]{1,0:T(1,128)}, f32[1,16]{1,0:T(1,128)S(1)}, u32[]{:S(2)}) %copy-start.15) | copy-done | bytes 88
  29.3 3.5 %write_out.1 = (f32[3,8,32,128]{3,2,1,0:T(8,128)}, f32[3,8,32,128]{3,2,1,0:T(8,128)}, f32[16,8,32,128]{3,2,1,0:T(8,128)}, f32[1,16]{1,0:T(1,128)}) custom-call(f32[3,8,32,128]{3,2,1,0:T(8,128)} %copy-done.5, f32[3,8,32,128]{3,2,1,0:T(8,128)} %copy-done.6, f32[16,8,32,128]{3,2,1,0:T(8,128)} %copy-done.1, f32[1,16]{1,0:T(1,128)} %copy-done.15), custom_call_target="tpu_custom_call" | custom-call | tf_op jit(solution)/shard_map/write_out/pallas_call | solution.py:305
Async XLA Ops:
  0.6 1.6 %copy-start = (f32[16,8,32,128]{3,2,1,0:T(8,128)S(1)}, f32[16,8,32,128]{3,2,1,0:T(8,128)}, u32[]{:S(2)}) copy-start(f32[16,8,32,128]{3,2,1,0:T(8,128)} %dft_hbm.1) | copy-start | bytes 6291460
  2.2 1.0 %copy-start.2 = (f32[3,8,32,128]{3,2,1,0:T(8,128)S(1)}, f32[3,8,32,128]{3,2,1,0:T(8,128)}, u32[]{:S(2)}) copy-start(f32[3,8,32,128]{3,2,1,0:T(8,128)} %e_hbm.1) | copy-start | bytes 1179652
  3.2 1.0 %copy-start.3 = (f32[3,8,32,128]{3,2,1,0:T(8,128)S(1)}, f32[3,8,32,128]{3,2,1,0:T(8,128)}, u32[]{:S(2)}) copy-start(f32[3,8,32,128]{3,2,1,0:T(8,128)} %h_hbm.1) | copy-start | bytes 1179652
  4.2 1.0 %copy-start.4 = (f32[3,8,32,128]{3,2,1,0:T(8,128)S(1)}, f32[3,8,32,128]{3,2,1,0:T(8,128)}, u32[]{:S(2)}) copy-start(f32[3,8,32,128]{3,2,1,0:T(8,128)} %ef_hbm.1) | copy-start | bytes 1179652
  5.2 0.9 %copy-start.7 = (f32[8,32,128]{2,1,0:T(8,128)S(1)}, f32[8,32,128]{2,1,0:T(8,128)}, u32[]{:S(2)}) copy-start(f32[8,32,128]{2,1,0:T(8,128)} %ec_hbm.1) | copy-start | bytes 393220
  6.1 0.9 %copy-start.8 = (f32[8,32,128]{2,1,0:T(8,128)S(1)}, f32[8,32,128]{2,1,0:T(8,128)}, u32[]{:S(2)}) copy-start(f32[8,32,128]{2,1,0:T(8,128)} %hc_hbm.1) | copy-start | bytes 393220
  7.0 0.9 %copy-start.9 = (f32[4,2,32,128]{3,2,1,0:T(8,128)S(1)}, f32[4,2,32,128]{3,2,1,0:T(8,128)}, u32[]{:S(2)}) copy-start(f32[4,2,32,128]{3,2,1,0:T(8,128)} %modes_hbm.1) | copy-start | bytes 393220
  7.9 0.7 %copy-start.10 = (s32[1,1,16]{2,1,0:T(1,128)S(1)}, s32[1,1,16]{2,1,0:T(1,128)}, u32[]{:S(2)}) copy-start(s32[1,1,16]{2,1,0:T(1,128)} %mask_ref.1) | copy-start | bytes 196
  8.6 0.7 %copy-start.11 = (f32[8]{0:T(128)S(1)}, f32[8]{0:T(128)}, u32[]{:S(2)}) copy-start(f32[8]{0:T(128)} %omega_ref.1) | copy-start | bytes 100
  9.2 0.7 %copy-start.12 = (s32[4]{0:T(128)S(1)}, s32[4]{0:T(128)}, u32[]{:S(2)}) copy-start(s32[4]{0:T(128)} %pidx_ref.1) | copy-start | bytes 52
  9.9 0.7 %copy-start.13 = (s32[4]{0:T(128)S(1)}, s32[4]{0:T(128)}, u32[]{:S(2)}) copy-start(s32[4]{0:T(128)} %powner_ref.1) | copy-start | bytes 52
  10.6 0.7 %copy-start.14 = (f32[1,16]{1,0:T(1,128)S(1)}, f32[1,16]{1,0:T(1,128)}, u32[]{:S(2)}) copy-start(f32[1,16]{1,0:T(1,128)} %mon_ref.1) | copy-start | bytes 196
  25.9 1.3 %copy-start.1 = (f32[16,8,32,128]{3,2,1,0:T(8,128)}, f32[16,8,32,128]{3,2,1,0:T(8,128)S(1)}, u32[]{:S(2)}) copy-start(f32[16,8,32,128]{3,2,1,0:T(8,128)S(1)} %get-tuple-element.10.dn) | copy-start | bytes 6291460
  27.3 0.7 %copy-start.5 = (f32[3,8,32,128]{3,2,1,0:T(8,128)}, f32[3,8,32,128]{3,2,1,0:T(8,128)S(1)}, u32[]{:S(2)}) copy-start(f32[3,8,32,128]{3,2,1,0:T(8,128)S(1)} %get-tuple-element.8.en) | copy-start | bytes 1179652
  28.0 0.8 %copy-start.6 = (f32[3,8,32,128]{3,2,1,0:T(8,128)}, f32[3,8,32,128]{3,2,1,0:T(8,128)S(1)}, u32[]{:S(2)}) copy-start(f32[3,8,32,128]{3,2,1,0:T(8,128)S(1)} %get-tuple-element.9.hn) | copy-start | bytes 1179652
  28.8 0.5 %copy-start.15 = (f32[1,16]{1,0:T(1,128)}, f32[1,16]{1,0:T(1,128)S(1)}, u32[]{:S(2)}) copy-start(f32[1,16]{1,0:T(1,128)S(1)} %get-tuple-element.11.mon) | copy-start | bytes 196

commit v2 on v1

--- a/solution.py
+++ b/solution.py
@@ -35,9 +35,9 @@
 
 def step(
     sizes, e_hbm, h_hbm, ef_hbm, ec_hbm, hc_hbm, dft_hbm, modes_hbm,
-    mask_ref, omega_ref, pidx_ref, powner_ref, mon_ref,
+    mask_hbm, omega_hbm, pidx_hbm, powner_hbm, mon_hbm,
     en, hn, dn, mon_out,
-    ef, ec, hc, modes,
+    ef, ec, hc, modes, mask_ref, omega_ref, pidx_ref, powner_ref, mon_ref,
     hx_in, hy_in, hz_in, ex_in, ey_in, ez_in, hy_out, ey_out, mine, rows,
     load_sems, h_send, h_recv, e_send, e_recv, all_send, all_recv,
 ):
@@ -60,7 +60,8 @@
     loads = [
         pltpu.make_async_copy(src, dst, load_sems.at[i])
         for i, (src, dst) in enumerate(
-            [(h_hbm, hn), (e_hbm, en), (ec_hbm, ec), (modes_hbm, modes), (hc_hbm, hc), (ef_hbm, ef), (dft_hbm, dn)]
+            [(h_hbm, hn), (e_hbm, en), (ec_hbm, ec), (modes_hbm, modes), (hc_hbm, hc), (ef_hbm, ef), (dft_hbm, dn),
+             (mask_hbm, mask_ref), (omega_hbm, omega_ref), (pidx_hbm, pidx_ref), (powner_hbm, powner_ref), (mon_hbm, mon_ref)]
         )
     ]
     for load in loads[:3]:
@@ -70,7 +71,7 @@
             barrier, inc=1, device_id=dev, device_id_type=pl.DeviceIdType.LOGICAL
         )
     )
-    for load in loads[3:]:
+    for load in loads[7:] + loads[3:7]:
         load.start()
 
     def remote(src, dst, send, recv, dev):
@@ -106,6 +107,8 @@
     for i in (0, 2, 1):
         pl.when(up[i][0])(h_copies[i].start)
 
+    for load in loads[7:]:
+        load.wait()
     sub8 = lax.broadcasted_iota(jnp.int32, (8, 128), 0)
     angle_rows = jnp.zeros((8, 128), jnp.float32)
     angle_lanes = jnp.zeros((8, 128), jnp.float32)
@@ -261,7 +264,7 @@
     f32 = jnp.float32
     hbm = pl.BlockSpec(memory_space=pltpu.HBM)
     vmem = pl.BlockSpec(memory_space=pltpu.VMEM)
-    smem = pl.BlockSpec(memory_space=pltpu.SMEM)
+    far = lambda x: pltpu.with_memory_space_constraint(x, pltpu.HBM)
     held = pl.pallas_call(
         functools.partial(step, sizes),
         out_shape=[
@@ -270,13 +273,18 @@
             pltpu.VMEM(dft_acc.shape, f32),
             pltpu.VMEM(monitor_acc.shape, f32),
         ],
-        in_specs=[hbm] * 7 + [smem] * 4 + [vmem],
+        in_specs=[hbm] * 12,
         out_specs=[vmem] * 4,
         scratch_shapes=[
             pltpu.VMEM(e_forward.shape, f32),
             pltpu.VMEM(e_coeff.shape, f32),
             pltpu.VMEM(h_coeff.shape, f32),
             pltpu.VMEM(port_modes.shape, f32),
+            pltpu.SMEM(design_mask.shape, jnp.int32),
+            pltpu.SMEM(omega_t.shape, f32),
+            pltpu.SMEM(port_index.shape, jnp.int32),
+            pltpu.SMEM(port_owner.shape, jnp.int32),
+            pltpu.VMEM(monitor_acc.shape, f32),
             pltpu.VMEM((2, nz, ny), f32),
             pltpu.VMEM((8, 128), f32),
             pltpu.VMEM((2, nx, ny), f32),
@@ -287,7 +295,7 @@
             pltpu.VMEM((8, 128), f32),
             pltpu.VMEM((1, 128), f32),
             pltpu.VMEM((n - 1, 1, 128), f32),
-            pltpu.SemaphoreType.DMA((7,)),
+            pltpu.SemaphoreType.DMA((12,)),
             pltpu.SemaphoreType.DMA((3,)),
             pltpu.SemaphoreType.DMA((3,)),
             pltpu.SemaphoreType.DMA((3,)),
@@ -299,8 +307,8 @@
             collective_id=0, has_side_effects=True, vmem_limit_bytes=24 * 2**20
         ),
         name="yee_step",
-    )(e_field, h_field, e_forward, e_coeff, h_coeff, dft_acc, port_modes,
-      design_mask, omega_t, port_index, port_owner, monitor_acc)
+    )(*map(far, (e_field, h_field, e_forward, e_coeff, h_coeff, dft_acc, port_modes,
+      design_mask, omega_t, port_index, port_owner, monitor_acc)))
     shape = lambda x: jax.ShapeDtypeStruct(x.shape, f32)
     return pl.pallas_call(
         write_out,
@@ -309,7 +317,7 @@
         out_specs=[hbm] * 4,
         scratch_shapes=[pltpu.SemaphoreType.DMA((7,))],
         name="write_out",
-    )(*held)
+    )(*[pltpu.with_memory_space_constraint(x, pltpu.VMEM) for x in held])
 
 
 def solution(mesh):

time: 33.2 us -> 16.1 us (0.48)
  local copies, waits for them, and re-layouts: 13.9 us -> 0 us
  Pallas kernels: 18.2 us -> 15.3 us
    unnamed x32 -> x0, local copies, waits for them, and re-layouts: 13.9 us -> none
    pallas_call x1, Pallas kernels: 3.48 us -> 1.63 us  [body(): pl.pallas_call(write_out, out_shape=[shape(x) for x in (e_field, h_field,...]
    pallas_call x1, Pallas kernels: 14.7 us -> 13.7 us  [body(): pl.pallas_call(functools.partial(step, sizes), out_shape=[pltpu.VMEM(e_fi...]
where the time goes in v2:
time: 16.1 us; the launch traced here: 15.9 us
  Pallas kernels  15.3 us (95%)
  between operations  0.64 us (4%)
    pallas_call x1, Pallas kernels, body(): pl.pallas_call(functools.partial(step, sizes), out_shape=[pltpu.VMEM(e_fi...  13.7 us
    pallas_call x1, Pallas kernels, body(): pl.pallas_call(write_out, out_shape=[shape(x) for x in (e_field, h_field,...  1.63 us

profile of v2, /device:TPU:0, one launch (start us, length us, event | category | flops | bytes accessed | tf_op | source)
XLA Modules:
  0.0 15.9 jit_solution(18222494849918539121)
XLA Ops:
  0.6 13.7 %yee_step.1 = (f32[3,8,32,128]{3,2,1,0:T(8,128)S(1)}, f32[3,8,32,128]{3,2,1,0:T(8,128)S(1)}, f32[16,8,32,128]{3,2,1,0:T(8,128)S(1)}, f32[1,16]{1,0:T(1,128)S(1)}) custom-call(f32[3,8,32,128]{3,2,1,0:T(8,128)} %e_hbm.1, f32[3,8,32,128]{3,2,1,0:T(8,128)} %h_hbm.1, f32[3,8,32,128]{3,2,1,0:T(8,128)} %ef_hbm.1, f32[8,32,128]{2,1,0:T(8,128)} %ec_hbm.1, ...), custom_call_target="tpu_custom_call" | custom-call | tf_op jit(solution)/shard_map/yee_step/pallas_call | solution.py:268
  14.3 1.6 %write_out.1 = (f32[3,8,32,128]{3,2,1,0:T(8,128)}, f32[3,8,32,128]{3,2,1,0:T(8,128)}, f32[16,8,32,128]{3,2,1,0:T(8,128)}, f32[1,16]{1,0:T(1,128)}) custom-call(f32[3,8,32,128]{3,2,1,0:T(8,128)S(1)} %get-tuple-element.8.en, f32[3,8,32,128]{3,2,1,0:T(8,128)S(1)} %get-tuple-element.9.hn, f32[16,8,32,128]{3,2,1,0:T(8,128)S(1)} %get-tuple-element.10.dn, ...), custom_call_target="tpu_custom_call" | custom-call | tf_op jit(solution)/shard_map/write_out/pallas_call | solution.py:313

commit v3 on v2

--- a/solution.py
+++ b/solution.py
@@ -39,7 +39,7 @@
     en, hn, dn, mon_out,
     ef, ec, hc, modes, mask_ref, omega_ref, pidx_ref, powner_ref, mon_ref,
     hx_in, hy_in, hz_in, ex_in, ey_in, ez_in, hy_out, ey_out, mine, rows,
-    load_sems, h_send, h_recv, e_send, e_recv, all_send, all_recv,
+    load_sems, h_send, h_recv, e_send, e_recv, all_send, all_recv, known_sems,
 ):
     n_gx, n_gy, n_gz = sizes
     n = n_gx * n_gy * n_gz
@@ -49,12 +49,11 @@
     nx, nz, ny = ec.shape
     zt = nz // 8
 
-    def each_other(run):
-        if n <= UNROLL:
-            for k in range(1, n):
-                run(k, lax.rem(me + k, n))
-        else:
-            lax.fori_loop(1, n, lambda k, _: (run(k, lax.rem(me + k, n)), 0)[1], 0)
+    lines = [(a, n_gx, stride_x), (b, n_gy, stride_y), (c, n_gz, 1)]
+    partners = [
+        [me + (lax.rem(at + k, size) - at) * stride for k in range(1, size)]
+        for at, size, stride in lines
+    ]
 
     barrier = pltpu.get_barrier_semaphore()
     loads = [
@@ -66,11 +65,11 @@
     ]
     for load in loads[:3]:
         load.start()
-    each_other(
-        lambda k, dev: pl.semaphore_signal(
-            barrier, inc=1, device_id=dev, device_id_type=pl.DeviceIdType.LOGICAL
-        )
-    )
+    for line in partners:
+        for dev in line:
+            pl.semaphore_signal(
+                barrier, inc=1, device_id=dev, device_id_type=pl.DeviceIdType.LOGICAL
+            )
     for load in loads[7:] + loads[3:7]:
         load.start()
 
@@ -103,9 +102,17 @@
     hy_out[...] = pack_lane(
         [hn[comp, x] for comp in (0, 2) for x in range(nx)], ny - 1, lane8
     )
-    pl.semaphore_wait(barrier, n - 1)
+    pl.semaphore_wait(barrier, sum(map(len, partners)))
     for i in (0, 2, 1):
         pl.when(up[i][0])(h_copies[i].start)
+
+    def tell(line, sem):
+        for dev in line:
+            pl.semaphore_signal(
+                sem, inc=1, device_id=dev, device_id_type=pl.DeviceIdType.LOGICAL
+            )
+
+    tell(partners[1], known_sems.at[0])
 
     for load in loads[7:]:
         load.wait()
@@ -138,6 +145,10 @@
         en[1, x] = en[1, x] - coef * (low(h0, 0) - d2)
         en[2, x] = en[2, x] - coef * (d1 - low(h0, 1))
 
+    if n_gy > 1:
+        pl.semaphore_wait(known_sems.at[0], n_gy - 1)
+    tell(partners[2], known_sems.at[1])
+
     for i, landing in enumerate((hx_in, hy_in, hz_in)):
         pl.when(down[i][0])(h_copies[i].wait_recv)
 
@@ -173,12 +184,16 @@
         total = jnp.sum(jnp.sum(total, axis=0, keepdims=True), axis=1, keepdims=True)
         total = jnp.where(inside, total, 0.0)
         share = jnp.where(lane8 == p, total, share)
+
     mine[...] = share[0:1]
-
-    def send_row(k, dev):
-        remote(mine, rows.at[k - 1], all_send, all_recv, dev).start()
-
-    each_other(send_row)
+    if n_gz > 1:
+        pl.semaphore_wait(known_sems.at[1], n_gz - 1)
+
+    def send_row(k, _):
+        remote(mine, rows.at[k - 1], all_send, all_recv, lax.rem(me + k, n)).start()
+        return 0
+
+    lax.fori_loop(1, n, send_row, 0, unroll=n <= UNROLL)
     for i in (0, 2):
         pl.when(down[i][0])(e_copies[i].start)
     ey_out[...] = pack_lane([en[comp, x] for comp in (0, 2) for x in range(nx)], 0, lane8)
@@ -259,8 +274,8 @@
 
 def body(sizes, e_field, h_field, e_forward, e_coeff, h_coeff, dft_acc, design_mask,
          omega_t, port_index, port_owner, port_modes, monitor_acc):
+    nx, nz, ny = e_coeff.shape
     n = sizes[0] * sizes[1] * sizes[2]
-    nx, nz, ny = e_coeff.shape
     f32 = jnp.float32
     hbm = pl.BlockSpec(memory_space=pltpu.HBM)
     vmem = pl.BlockSpec(memory_space=pltpu.VMEM)
@@ -302,6 +317,7 @@
             pltpu.SemaphoreType.DMA((3,)),
             pltpu.SemaphoreType.DMA,
             pltpu.SemaphoreType.DMA,
+            pltpu.SemaphoreType.REGULAR((2,)),
         ],
         compiler_params=pltpu.CompilerParams(
             collective_id=0, has_side_effects=True, vmem_limit_bytes=24 * 2**20

time: 16.1 us -> 15.5 us (0.963)
  Pallas kernels: 15.3 us -> 14.7 us
    pallas_call x1, Pallas kernels: 13.7 us -> 13.1 us  [body(): pl.pallas_call(functools.partial(step, sizes), out_shape=[pltpu.VMEM(e_fi...]
where the time goes in v3:
time: 15.5 us; the launch traced here: 15.4 us
  Pallas kernels  14.7 us (95%)
  between operations  0.64 us (4%)
    pallas_call x1, Pallas kernels, body(): pl.pallas_call(functools.partial(step, sizes), out_shape=[pltpu.VMEM(e_fi...  13.1 us
    pallas_call x1, Pallas kernels, body(): pl.pallas_call(write_out, out_shape=[shape(x) for x in (e_field, h_field,...  1.63 us

profile of v3, /device:TPU:0, one launch (start us, length us, event | category | flops | bytes accessed | tf_op | source)
XLA Modules:
  0.0 15.4 jit_solution(1090504879298068652)
XLA Ops:
  0.6 13.1 %yee_step.1 = (f32[3,8,32,128]{3,2,1,0:T(8,128)S(1)}, f32[3,8,32,128]{3,2,1,0:T(8,128)S(1)}, f32[16,8,32,128]{3,2,1,0:T(8,128)S(1)}, f32[1,16]{1,0:T(1,128)S(1)}) custom-call(f32[3,8,32,128]{3,2,1,0:T(8,128)} %e_hbm.1, f32[3,8,32,128]{3,2,1,0:T(8,128)} %h_hbm.1, f32[3,8,32,128]{3,2,1,0:T(8,128)} %ef_hbm.1, f32[8,32,128]{2,1,0:T(8,128)} %ec_hbm.1, ...), custom_call_target="tpu_custom_call" | custom-call | tf_op jit(solution)/shard_map/yee_step/pallas_call | solution.py:283
  13.7 1.6 %write_out.1 = (f32[3,8,32,128]{3,2,1,0:T(8,128)}, f32[3,8,32,128]{3,2,1,0:T(8,128)}, f32[16,8,32,128]{3,2,1,0:T(8,128)}, f32[1,16]{1,0:T(1,128)}) custom-call(f32[3,8,32,128]{3,2,1,0:T(8,128)S(1)} %get-tuple-element.8.en, f32[3,8,32,128]{3,2,1,0:T(8,128)S(1)} %get-tuple-element.9.hn, f32[16,8,32,128]{3,2,1,0:T(8,128)S(1)} %get-tuple-element.10.dn, ...), custom_call_target="tpu_custom_call" | custom-call | tf_op jit(solution)/shard_map/write_out/pallas_call | solution.py:329
